TPU v7x, 128 devices: a whole 4x4x4 slice. The times are simulated.
128 devices in a mesh: aux: 4 (over x), pair: 32 (over z, y, core).
Axes of the slice: x: 4, y: 4, z: 4, core: 2. Of those that a mesh axis runs over, the one named last changes fastest.
Arguments:
- three_index: bfloat16 [512, 256, 2048], P('pair', None, 'aux'), may hold values from -0.875 to 0.875
- fock_diag: float32 [512], replicated, may hold values from -1.2 to -0.3
- pair_occ: int32 [992, 2], P('pair'), may hold values from 0 to 511, as said below
- pno_count: int32 [992], P('pair'), may hold values from 32 to 128
- pno_energy: float32 [992, 128], P('pair'), may hold values from 0.3 to 3
- pno_coef: bfloat16 [992, 2, 256, 128], P('pair'), may hold values from -0.375 to 0.375
Outputs:
- pair_energy: float32 [992], P('pair')
- grad_ints: float32 [512, 256, 2048], P('pair', None, 'aux')
Inputs may be any that keep to these rules, and one draw needn't show every extreme that they name: `pair_occ`: orbital o belongs to the block o // 16. Among the 62 orbitals named by the pairs of one aligned block of 31 rows, at most 2 belong to any one orbital block, and one orbital block receives exactly 2 from every such row block; i may equal j.
All inputs are finite; a program needn't handle non-finite values.
Results may differ from a plain program's by a relative error of at most 0.0061.
Values may be sent and summed in bfloat16 or wider, within the bound.
A program may use at most 128 MiB of HBM per device.

v0:
```python
import jax
import jax.numpy as jnp
from jax import lax
from jax.sharding import PartitionSpec as P


def local(three_index, fock_diag, pair_occ, pno_count, pno_energy, pno_coef):
    groups = lax.axis_size("pair")
    occ_dev = three_index.shape[0]
    width_dom = three_index.shape[1]
    width_aux = three_index.shape[2]
    pair_dev = pair_occ.shape[0]
    width_pno = pno_coef.shape[3]
    halves = 2 * pair_dev
    capacity = max(2, halves // groups + 1)
    slots = groups * capacity
    occ_flat = pair_occ.reshape(halves)
    owner_of = occ_flat // occ_dev
    local_index = occ_flat % occ_dev
    owner_hot = (owner_of[:, None] == jnp.arange(groups, dtype=jnp.int32)[None, :]).astype(
        jnp.int32
    )
    before = jnp.cumsum(owner_hot, axis=0) - owner_hot
    rank_in = jnp.sum(before * owner_hot, axis=1)
    slot_of = owner_of * capacity + rank_in
    request = jnp.zeros((slots,), jnp.int32).at[slot_of].set(local_index + 1)
    arrived = lax.all_to_all(
        request.reshape(groups, capacity), "pair", split_axis=0, concat_axis=0, tiled=True
    ).reshape(slots)
    is_live = arrived > 0
    row_index = jnp.maximum(arrived - 1, 0)
    selected = jnp.take(three_index, row_index, axis=0)
    selected = jnp.where(is_live[:, None, None], selected, jnp.zeros_like(selected))
    coef_half = pno_coef.reshape(halves, width_dom, width_pno)
    rows_back = lax.all_to_all(
        selected.reshape(groups, capacity, width_dom, width_aux),
        "pair",
        split_axis=0,
        concat_axis=0,
        tiled=True,
    )
    mine = jnp.take(rows_back.reshape(slots, width_dom, width_aux), slot_of, axis=0)
    projected = jnp.einsum(
        "hdp,hdq->hpq", coef_half, mine, preferred_element_type=jnp.float32
    ).astype(jnp.bfloat16)
    paired = projected.reshape(pair_dev, 2, width_pno, width_aux)
    rows_i = paired[:, 0]
    rows_j = paired[:, 1]
    partial_sum = jnp.einsum("kpq,krq->kpr", rows_i, rows_j, preferred_element_type=jnp.float32)
    coupling = lax.psum(partial_sum, "aux")
    fock_i = jnp.take(fock_diag, pair_occ[:, 0])
    fock_j = jnp.take(fock_diag, pair_occ[:, 1])
    denom = pno_energy[:, :, None] + pno_energy[:, None, :] - (fock_i + fock_j)[:, None, None]
    in_pno = jnp.arange(width_pno, dtype=jnp.int32)[None, :] < pno_count[:, None]
    both_in = in_pno[:, :, None] & in_pno[:, None, :]
    amplitude = jnp.where(both_in, -coupling / denom, jnp.float32(0.0))
    mixed = 2.0 * amplitude - jnp.swapaxes(amplitude, 1, 2)
    energy = jnp.sum(coupling * mixed, axis=(1, 2)) / (width_pno * width_pno)
    weights = mixed.astype(jnp.bfloat16)
    gamma_i = jnp.einsum(
        "kab,kbq->kaq", weights, rows_j, preferred_element_type=jnp.float32
    ).astype(jnp.bfloat16)
    gamma_j = jnp.einsum(
        "kba,kbq->kaq", weights, rows_i, preferred_element_type=jnp.float32
    ).astype(jnp.bfloat16)
    gamma = jnp.stack([gamma_i, gamma_j], axis=1).reshape(halves, width_pno, width_aux)
    dom_terms = jnp.einsum(
        "hdp,hpq->hdq", coef_half, gamma, preferred_element_type=jnp.float32
    ).astype(jnp.bfloat16)
    term_send = jnp.zeros((slots, width_dom, width_aux), jnp.bfloat16).at[slot_of].set(dom_terms)
    terms = lax.all_to_all(
        term_send.reshape(groups, capacity, width_dom, width_aux),
        "pair",
        split_axis=0,
        concat_axis=0,
        tiled=True,
    )
    terms = terms.reshape(slots, width_dom, width_aux)
    occ_hot = (row_index[None, :] == jnp.arange(occ_dev, dtype=jnp.int32)[:, None]) & is_live[
        None, :
    ]
    grad = jnp.dot(
        occ_hot.astype(jnp.bfloat16),
        terms.reshape(slots, width_dom * width_aux),
        preferred_element_type=jnp.float32,
    )
    return (energy, grad.reshape(occ_dev, width_dom, width_aux))


def solution(mesh):
    placed = (
        P("pair", None, "aux"),
        P(),
        P("pair", None),
        P("pair"),
        P("pair", None),
        P("pair", None, None, None),
    )
    return jax.shard_map(
        local,
        mesh=mesh,
        in_specs=placed,
        out_specs=(P("pair"), P("pair", None, "aux")),
        check_vma=False,
    )
```

profile of v0, /device:TPU:0, one launch (start us, length us, event | category | flops | bytes accessed | tf_op | source)
XLA Modules:
  0.0 715.7 jit_solution(3268946440946229828)
XLA Ops:
  7.2 0.0 copy-start
  7.2 0.8 copy.56
  8.0 0.1 reshape.245
  8.1 0.1 reshape.244
  8.2 0.1 fusion.14
  8.3 0.1 reduce_window_sum.11
  8.4 0.2 select_reduce_fusion
  8.6 0.8 scatter_custom_fusion
  9.3 0.1 all_to_all.12
  9.4 15.6 %all_to_all.19 = s32[32,1,2]{2,1,0:T(1,128)S(1)} all-to-all(s32[32,1,2]{2,1,0:T(1,128)S(1)} %bitcast.90), channel_id=1, replica_groups=mesh['aux'=4,'pair'=32] {'pair'}, dimensions={0} | all-to-all | bytes 512 | tf_op jit(solution)/shard_map/all_to_all | solution.py:27
  25.0 0.1 copy.59
  25.1 0.1 copy.62
  25.2 0.1 copy.60
  25.3 0.1 copy.63
  25.4 0.1 reshape.269
  25.5 9.8 %gather_fusion = bf16[64,256,512]{2,1,0:T(8,128)(2,1)} fusion(bf16[16,256,512]{2,1,0:T(8,128)(2,1)} %param.8, s32[1024]{0:T(1024)S(1)} %pad_clamp_fusion.3), kind=kCustom, calls=%fused_computation.2 | custom fusion | bytes 33554688 | tf_op jit(solution)/shard_map/jit(_take)/gather | solution.py:32
  35.3 14.3 %select_select_fusion = bf16[32,2,256,512]{3,2,1,0:T(8,128)(2,1)} fusion(bf16[32,2,256,512]{3,2,1,0:T(8,128)(2,1)} %bitcast.81, pred[32,2]{1,0:T(8,128)(4,1)S(1)} %copy.62, pred[32,2]{1,0:T(8,128)(4,1)S(1)} %copy.60), kind=kLoop, calls=%fused_computation.9 | loop fusion | flops 16777216 | bytes 33554560 | tf_op jit(solution)/shard_map/jit(_where)/select_n | solution.py:33
  49.6 5.2 all-to-all-start.1
  54.8 0.2 all-reduce.2.cloned.1.call-start
  55.0 213.0 %all-to-all-done.1 = bf16[32,2,256,512]{3,2,1,0:T(8,128)(2,1)} async-done(((bf16[32,2,256,512]{3,2,1,0:T(8,128)(2,1)}), bf16[32,2,256,512]{3,2,1,0:T(8,128)(2,1)}, u32[]{:S(2)}, u32[]{:S(2)}) %all-to-all-start.1) | async-done | bytes 16777248 | tf_op jit(solution)/shard_map/all_to_all | solution.py:35
  268.0 13.3 %gather_fusion.1 = bf16[62,256,512]{2,1,0:T(8,128)(2,1)} fusion(bf16[64,256,512]{2,1,0:T(8,128)(2,1)} %bitcast.6, s32[1024]{0:T(1024)S(1)} %pad_clamp_fusion.2), kind=kCustom, calls=%fused_computation.3 | custom fusion | bytes 32506104 | tf_op jit(solution)/shard_map/jit(_take)/gather | solution.py:42
  281.3 11.8 %fusion.7 = bf16[62,512,128]{2,1,0:T(8,128)(2,1)} fusion(bf16[62,256,128]{2,1,0:T(8,128)(2,1)} %bitcast.83, bf16[62,256,512]{2,1,0:T(8,128)(2,1)} %gather_fusion.1, pred[62]{0:T(512)(128)(4,1)S(1)} %compare_and_fusion), kind=kOutput, calls=%fused_computation.16 | convolution fusion | flops 2092564480 | bytes 28442686 | tf_op jit(solution)/shard_map/hdp,hdq->hpq/dot_general | solution.py:43
  293.1 6.0 fusion.11
  299.1 0.0 all-reduce.2.cloned.1.call-update
  299.1 0.0 copy-done.3
  299.2 0.7 gather_fusion.3
  299.9 0.7 gather_fusion.2
  300.6 0.1 iota_compare_fusion.1
  300.7 52.8 %all-reduce.2.cloned.1.call-done = f32[31,128,128]{2,1,0:T(8,128)} async-done(((f32[31,128,128]{2,1,0:T(8,128)}), f32[31,128,128]{2,1,0:T(8,128)}) %all-reduce.2.cloned.1.call-update) | async-done | bytes 2031632 | tf_op jit(solution)/shard_map/psum | solution.py:50
  353.5 2.3 copy.67
  355.8 2.7 broadcast_multiply_fusion
  358.5 2.9 copy.68
  361.4 4.0 fusion.13
  365.3 5.5 convert_bitcast_fusion.1
  370.8 3.2 convert_bitcast_fusion.2
  374.0 4.1 pad_maximum_fusion
  378.2 4.3 copy.71
  382.4 11.3 %convert_bitcast_fusion = bf16[62,256,512]{1,2,0:T(8,128)(2,1)} fusion(bf16[62,128,512]{2,1,0:T(8,128)(2,1)} %bitcast.82, bf16[62,256,128]{2,1,0:T(8,128)(2,1)} %bitcast.84), kind=kOutput, calls=%fused_computation.10 | convolution fusion | flops 2088501248 | bytes 28442624 | tf_op jit(solution)/shard_map/hdp,hpq->hdq/dot_general | solution.py:67
  393.7 21.9 %copy.73 = bf16[62,256,512]{2,1,0:T(8,128)(2,1)} copy(bf16[62,256,512]{1,2,0:T(8,128)(2,1)} %convert_bitcast_fusion) | data formatting | bytes 32505856 | tf_op jit(solution)/shard_map/convert_element_type | solution.py:69
  415.6 5.9 broadcast.266
  421.5 41.9 %scatter_fusion = bf16[64,256,512]{2,1,0:T(8,128)(2,1)} fusion(bf16[64,256,512]{2,1,0:T(8,128)(2,1)} %broadcast.266, s32[62]{0:T(128)S(1)} %fusion.22, bf16[62,256,512]{2,1,0:T(8,128)(2,1)} %copy.73), kind=kCustom, calls=%fused_computation.5 | custom fusion | bytes 48759032 | tf_op jit(solution)/shard_map/scatter | solution.py:70
  463.4 7.3 %all-to-all-start.2 = ((bf16[32,2,256,512]{3,2,1,0:T(8,128)(2,1)}), bf16[32,2,256,512]{3,2,1,0:T(8,128)(2,1)}, u32[]{:S(2)}, u32[]{:S(2)}) async-start(bf16[32,2,256,512]{3,2,1,0:T(8,128)(2,1)} %bitcast.80), calls=%async_computation.2 | async-start | bytes 33554432 | tf_op jit(solution)/shard_map/all_to_all | solution.py:71
  470.6 0.1 copy.69
  470.7 0.1 gt.19
  470.9 0.5 broadcast_multiply_fusion.1
  471.4 212.5 %all-to-all-done.2 = bf16[32,2,256,512]{3,2,1,0:T(8,128)(2,1)} async-done(((bf16[32,2,256,512]{3,2,1,0:T(8,128)(2,1)}), bf16[32,2,256,512]{3,2,1,0:T(8,128)(2,1)}, u32[]{:S(2)}, u32[]{:S(2)}) %all-to-all-start.2) | async-done | bytes 16777248 | tf_op jit(solution)/shard_map/all_to_all | solution.py:71
  683.9 16.8 %fusion = f32[16,256,512]{2,0,1:T(8,128)S(1)} fusion(s32[64]{0:T(128)S(1)} %reshape.269, pred[64]{0:T(512)(128)(4,1)S(1)} %gt.19, bf16[8,8,256,512]{3,2,1,0:T(8,128)(2,1)} %bitcast.32), kind=kOutput, calls=%fused_computation.6 | convolution fusion | flops 268437504 | bytes 25166144 | tf_op jit(solution)/shard_map/dot_general | solution.py:82
  700.6 8.3 %copy.75 = f32[16,256,512]{2,1,0:T(8,128)} copy(f32[16,256,512]{2,0,1:T(8,128)S(1)} %fusion) | data formatting | bytes 16777216
  (23 shorter events, 0.1 us)
Async XLA Ops:
  7.2 292.0 %copy-start = (f32[512]{0:T(512)S(1)}, f32[512]{0:T(512)}, u32[]{:S(2)}) copy-start(f32[512]{0:T(512)} %param.9) | copy-start | bytes 6148
  49.6 218.4 %all-to-all-start.1 = ((bf16[32,2,256,512]{3,2,1,0:T(8,128)(2,1)}), bf16[32,2,256,512]{3,2,1,0:T(8,128)(2,1)}, u32[]{:S(2)}, u32[]{:S(2)}) async-start(bf16[32,2,256,512]{3,2,1,0:T(8,128)(2,1)} %select_select_fusion), calls=%async_computation.1 | async-start | bytes 33554432 | tf_op jit(solution)/shard_map/all_to_all | solution.py:35
  54.8 298.7 %all-reduce.2.cloned.1.call-start = ((), (), s32[]{:S(2)}) async-start(), calls=%async_computation.3 | async-start | bytes 4063232 | tf_op jit(solution)/shard_map/psum | solution.py:50
  293.1 6.0 copy-start.3
  293.1 7.5 %copy-start.4 = (s32[31]{0:T(128)S(1)}, s32[31]{0:T(128)}, u32[]{:S(2)}) copy-start(s32[31]{0:T(128)} %param.11) | copy-start | bytes 376
  293.1 62.7 %copy-start.2 = (f32[31,128]{1,0:T(8,128)S(1)}, f32[31,128]{1,0:T(8,128)}, u32[]{:S(2)}) copy-start(f32[31,128]{1,0:T(8,128)} %param.12) | copy-start | bytes 47620
  361.4 9.5 %slice-start = ((s8[8126464]{0:T(1024)(128)(4,1)}), s8[4194304]{0:T(1024)(128)(4,1)S(1)}, s32[]{:S(2)}) async-start(s8[8126464]{0:T(1024)(128)(4,1)} %bitcast.87), calls=%async_computation.4 | async-start | bytes 8388608
  365.3 5.5 slice-start.1
  463.4 220.5 %all-to-all-start.2 = ((bf16[32,2,256,512]{3,2,1,0:T(8,128)(2,1)}), bf16[32,2,256,512]{3,2,1,0:T(8,128)(2,1)}, u32[]{:S(2)}, u32[]{:S(2)}) async-start(bf16[32,2,256,512]{3,2,1,0:T(8,128)(2,1)} %bitcast.80), calls=%async_computation.2 | async-start | bytes 33554432 | tf_op jit(solution)/shard_map/all_to_all | solution.py:71
  683.8 25.0 %copy-start.1 = (f32[512]{0:T(512)S(1)}, f32[512]{0:T(512)}, u32[]{:S(2)}) copy-start(f32[512]{0:T(512)} %param.9) | copy-start | bytes 6148
Sparse Core Ops, SparseCore 0:
  299.2 54.1 all-reduce.1
where the time goes:
time: 717 us; the launch traced here: 716 us
  waiting for transfers between devices  478 us (67%)
  local copies, waits for them, and re-layouts  114 us (16%)
  matrix products  54.5 us (8%)
  other arithmetic  26.1 us (4%)
  blocking collectives  15.6 us (2%)
  between operations  14.2 us (2%)
  starting transfers between devices  12.6 us (2%)
    all_to_all x1, waiting for transfers between devices, local(): lax.all_to_all(selected.reshape(groups, capacity, width_dom, width_aux),...  213 us
    all_to_all x1, waiting for transfers between devices, local(): lax.all_to_all(term_send.reshape(groups, capacity, width_dom, width_aux),...  212 us
    psum x1, waiting for transfers between devices, local(): coupling = lax.psum(partial_sum, 'aux')  52.8 us
    scatter x1, local copies, waits for them, and re-layouts, local(): jnp.zeros((slots, width_dom, width_aux), jnp.bfloat16).at[slot_of]  41.9 us
    convert_element_type x1, local copies, waits for them, and re-layouts, local(): dom_terms = jnp.einsum('hdp,hpq->hdq', coef_half, gamma, preferred_elemen...  21.9 us
    dot_general x1, matrix products, local(): jnp.dot(occ_hot.astype(jnp.bfloat16), terms.reshape(slots, width_dom * wi...  16.8 us
    all_to_all x1, blocking collectives, local(): lax.all_to_all(request.reshape(groups, capacity), 'pair', split_axis=0, c...  15.6 us
  transfers between devices with their start and end apart: 3, of which 3 were waited for; matrix products, arithmetic and copies ran while one was open for 0% of the time, Pallas kernels for 0%

commit v1 on v0

--- a/solution.py
+++ b/solution.py
@@ -47,7 +47,7 @@
     rows_i = paired[:, 0]
     rows_j = paired[:, 1]
     partial_sum = jnp.einsum("kpq,krq->kpr", rows_i, rows_j, preferred_element_type=jnp.float32)
-    coupling = lax.psum(partial_sum, "aux")
+    coupling = jnp.sum(lax.all_gather(partial_sum, "aux"), axis=0)
     fock_i = jnp.take(fock_diag, pair_occ[:, 0])
     fock_j = jnp.take(fock_diag, pair_occ[:, 1])
     denom = pno_energy[:, :, None] + pno_energy[:, None, :] - (fock_i + fock_j)[:, None, None]

time: 717 us -> 745 us (1.039)
  waiting for transfers between devices: 478 us -> 502 us
    all_gather x0 -> x1, waiting for transfers between devices: none -> 76.1 us  [local(): coupling = jnp.sum(lax.all_gather(partial_sum, 'aux'), axis=0)]
    psum x1 -> x0, waiting for transfers between devices: 52.8 us -> none  [local(): coupling = lax.psum(partial_sum, 'aux')]
    reduce_sum x0 -> x2, other arithmetic: none -> 8.39 us  [the longest x1 4.4 us: local(): coupling = jnp.sum(lax.all_gather(partial_sum, 'aux'), axis=0)]
where the time goes in v1:
time: 745 us; the launch traced here: 744 us
  waiting for transfers between devices  502 us (67%)
  local copies, waits for them, and re-layouts  114 us (15%)
  matrix products  54.6 us (7%)
  other arithmetic  31 us (4%)
  blocking collectives  15.6 us (2%)
  between operations  14.2 us (2%)
  starting transfers between devices  12.6 us (2%)
    all_to_all x1, waiting for transfers between devices, local(): lax.all_to_all(selected.reshape(groups, capacity, width_dom, width_aux),...  213 us
    all_to_all x1, waiting for transfers between devices, local(): lax.all_to_all(term_send.reshape(groups, capacity, width_dom, width_aux),...  212 us
    all_gather x1, waiting for transfers between devices, local(): coupling = jnp.sum(lax.all_gather(partial_sum, 'aux'), axis=0)  76.1 us
    scatter x1, local copies, waits for them, and re-layouts, local(): jnp.zeros((slots, width_dom, width_aux), jnp.bfloat16).at[slot_of]  41.9 us
    convert_element_type x1, local copies, waits for them, and re-layouts, local(): dom_terms = jnp.einsum('hdp,hpq->hdq', coef_half, gamma, preferred_elemen...  21.9 us
    dot_general x1, matrix products, local(): jnp.dot(occ_hot.astype(jnp.bfloat16), terms.reshape(slots, width_dom * wi...  16.8 us
    all_to_all x1, blocking collectives, local(): lax.all_to_all(request.reshape(groups, capacity), 'pair', split_axis=0, c...  15.6 us
  transfers between devices with their start and end apart: 3, of which 3 were waited for; matrix products, arithmetic and copies ran while one was open for 0% of the time, Pallas kernels for 0%

profile of v1, /device:TPU:0, one launch (start us, length us, event | category | flops | bytes accessed | tf_op | source)
XLA Modules:
  0.0 743.8 jit_solution(10553124941098850134)
XLA Ops:
  7.2 0.0 copy-start
  7.2 0.8 copy.58
  8.0 0.1 reshape.245
  8.1 0.1 reshape.244
  8.2 0.1 fusion.17
  8.3 0.1 reduce_window_sum.11
  8.4 0.2 select_reduce_fusion
  8.6 0.8 scatter_custom_fusion
  9.3 0.1 all_to_all.12
  9.4 15.6 %all_to_all.19 = s32[32,1,2]{2,1,0:T(1,128)S(1)} all-to-all(s32[32,1,2]{2,1,0:T(1,128)S(1)} %bitcast.91), channel_id=1, replica_groups=mesh['aux'=4,'pair'=32] {'pair'}, dimensions={0} | all-to-all | bytes 512 | tf_op jit(solution)/shard_map/all_to_all | solution.py:27
  25.0 0.1 copy.61
  25.1 0.1 copy.64
  25.2 0.1 copy.62
  25.3 0.1 copy.65
  25.4 0.1 reshape.269
  25.5 9.8 %gather_fusion = bf16[64,256,512]{2,1,0:T(8,128)(2,1)} fusion(bf16[16,256,512]{2,1,0:T(8,128)(2,1)} %param.8, s32[1024]{0:T(1024)S(1)} %pad_clamp_fusion.3), kind=kCustom, calls=%fused_computation.2 | custom fusion | bytes 33554688 | tf_op jit(solution)/shard_map/jit(_take)/gather | solution.py:32
  35.3 14.3 %select_select_fusion = bf16[32,2,256,512]{3,2,1,0:T(8,128)(2,1)} fusion(bf16[32,2,256,512]{3,2,1,0:T(8,128)(2,1)} %bitcast.81, pred[32,2]{1,0:T(8,128)(4,1)S(1)} %copy.64, pred[32,2]{1,0:T(8,128)(4,1)S(1)} %copy.62), kind=kLoop, calls=%fused_computation.9 | loop fusion | flops 16777216 | bytes 33554560 | tf_op jit(solution)/shard_map/jit(_where)/select_n | solution.py:33
  49.6 5.2 all-to-all-start.1
  54.8 0.2 all-gather.3.cloned.1.call-start
  55.0 213.0 %all-to-all-done.1 = bf16[32,2,256,512]{3,2,1,0:T(8,128)(2,1)} async-done(((bf16[32,2,256,512]{3,2,1,0:T(8,128)(2,1)}), bf16[32,2,256,512]{3,2,1,0:T(8,128)(2,1)}, u32[]{:S(2)}, u32[]{:S(2)}) %all-to-all-start.1) | async-done | bytes 16777248 | tf_op jit(solution)/shard_map/all_to_all | solution.py:35
  268.0 13.3 %gather_fusion.1 = bf16[62,256,512]{2,1,0:T(8,128)(2,1)} fusion(bf16[64,256,512]{2,1,0:T(8,128)(2,1)} %bitcast.6, s32[1024]{0:T(1024)S(1)} %pad_clamp_fusion.2), kind=kCustom, calls=%fused_computation.3 | custom fusion | bytes 32506104 | tf_op jit(solution)/shard_map/jit(_take)/gather | solution.py:42
  281.3 11.8 %fusion.7 = bf16[62,512,128]{2,1,0:T(8,128)(2,1)} fusion(bf16[62,256,128]{2,1,0:T(8,128)(2,1)} %bitcast.83, bf16[62,256,512]{2,1,0:T(8,128)(2,1)} %gather_fusion.1, pred[62]{0:T(512)(128)(4,1)S(1)} %compare_and_fusion), kind=kOutput, calls=%fused_computation.16 | convolution fusion | flops 2092564480 | bytes 28442686 | tf_op jit(solution)/shard_map/hdp,hdq->hpq/dot_general | solution.py:43
  293.1 6.1 fusion.11
  299.2 0.0 all-gather.3.cloned.1.call-update
  299.2 0.7 gather_fusion.3
  300.0 0.7 gather_fusion.2
  300.7 0.1 iota_compare_fusion.1
  300.8 76.1 %all-gather.3.cloned.1.call-done = f32[124,128,128]{2,1,0:T(8,128)} async-done(((f32[31,128,128]{2,1,0:T(8,128)}), f32[124,128,128]{2,1,0:T(8,128)}) %all-gather.3.cloned.1.call-update) | async-done | bytes 8126480 | tf_op jit(solution)/shard_map/all_gather | solution.py:50
  376.9 4.4 reduce_sum.31
  381.3 2.1 copy.69
  383.4 3.1 neg.7
  386.5 2.9 copy.70
  389.4 4.0 multiply_reduce_fusion
  393.4 5.4 convert_bitcast_fusion.2
  398.8 3.2 convert_bitcast_fusion.1
  402.1 4.1 pad_maximum_fusion
  406.2 4.3 copy.73
  410.5 11.3 %convert_bitcast_fusion = bf16[62,256,512]{1,2,0:T(8,128)(2,1)} fusion(bf16[62,128,512]{2,1,0:T(8,128)(2,1)} %bitcast.82, bf16[62,256,128]{2,1,0:T(8,128)(2,1)} %bitcast.84), kind=kOutput, calls=%fused_computation.10 | convolution fusion | flops 2088501248 | bytes 28442624 | tf_op jit(solution)/shard_map/hdp,hpq->hdq/dot_general | solution.py:67
  421.8 21.9 %copy.75 = bf16[62,256,512]{2,1,0:T(8,128)(2,1)} copy(bf16[62,256,512]{1,2,0:T(8,128)(2,1)} %convert_bitcast_fusion) | data formatting | bytes 32505856 | tf_op jit(solution)/shard_map/convert_element_type | solution.py:69
  443.6 5.9 broadcast.272
  449.5 41.9 %scatter_fusion = bf16[64,256,512]{2,1,0:T(8,128)(2,1)} fusion(bf16[64,256,512]{2,1,0:T(8,128)(2,1)} %broadcast.272, s32[62]{0:T(128)S(1)} %fusion.25, bf16[62,256,512]{2,1,0:T(8,128)(2,1)} %copy.75), kind=kCustom, calls=%fused_computation.5 | custom fusion | bytes 48759032 | tf_op jit(solution)/shard_map/scatter | solution.py:70
  491.4 7.3 all-to-all-start.2
  498.7 0.1 copy.71
  498.8 0.1 gt.19
  498.9 0.5 broadcast_multiply_fusion
  499.4 212.5 %all-to-all-done.2 = bf16[32,2,256,512]{3,2,1,0:T(8,128)(2,1)} async-done(((bf16[32,2,256,512]{3,2,1,0:T(8,128)(2,1)}), bf16[32,2,256,512]{3,2,1,0:T(8,128)(2,1)}, u32[]{:S(2)}, u32[]{:S(2)}) %all-to-all-start.2) | async-done | bytes 16777248 | tf_op jit(solution)/shard_map/all_to_all | solution.py:71
  711.9 16.8 %fusion = f32[16,256,512]{2,0,1:T(8,128)S(1)} fusion(s32[64]{0:T(128)S(1)} %reshape.269, pred[64]{0:T(512)(128)(4,1)S(1)} %gt.19, bf16[8,8,256,512]{3,2,1,0:T(8,128)(2,1)} %bitcast.33), kind=kOutput, calls=%fused_computation.6 | convolution fusion | flops 268437504 | bytes 25166144 | tf_op jit(solution)/shard_map/dot_general | solution.py:82
  728.7 8.3 %copy.77 = f32[16,256,512]{2,1,0:T(8,128)} copy(f32[16,256,512]{2,0,1:T(8,128)S(1)} %fusion) | data formatting | bytes 16777216
  (24 shorter events, 0.1 us)
Async XLA Ops:
  7.2 292.1 %copy-start = (f32[512]{0:T(512)S(1)}, f32[512]{0:T(512)}, u32[]{:S(2)}) copy-start(f32[512]{0:T(512)} %param.9) | copy-start | bytes 6148
  49.6 218.4 %all-to-all-start.1 = ((bf16[32,2,256,512]{3,2,1,0:T(8,128)(2,1)}), bf16[32,2,256,512]{3,2,1,0:T(8,128)(2,1)}, u32[]{:S(2)}, u32[]{:S(2)}) async-start(bf16[32,2,256,512]{3,2,1,0:T(8,128)(2,1)} %select_select_fusion), calls=%async_computation.1 | async-start | bytes 33554432 | tf_op jit(solution)/shard_map/all_to_all | solution.py:35
  54.8 322.1 %all-gather.3.cloned.1.call-start = ((), (), s32[]{:S(2)}) async-start(), calls=%async_computation.3 | async-start | bytes 10158080 | tf_op jit(solution)/shard_map/all_gather | solution.py:50
  293.1 6.1 copy-start.3
  293.1 7.6 %copy-start.4 = (s32[31]{0:T(128)S(1)}, s32[31]{0:T(128)}, u32[]{:S(2)}) copy-start(s32[31]{0:T(128)} %param.11) | copy-start | bytes 376
  381.3 8.1 %copy-start.2 = (f32[31,128]{1,0:T(8,128)S(1)}, f32[31,128]{1,0:T(8,128)}, u32[]{:S(2)}) copy-start(f32[31,128]{1,0:T(8,128)} %param.12) | copy-start | bytes 47620
  389.4 9.4 %slice-start = ((s8[8126464]{0:T(1024)(128)(4,1)}), s8[4194304]{0:T(1024)(128)(4,1)S(1)}, s32[]{:S(2)}) async-start(s8[8126464]{0:T(1024)(128)(4,1)} %bitcast.88), calls=%async_computation.4 | async-start | bytes 8388608
  393.4 5.4 slice-start.1
  491.4 220.5 %all-to-all-start.2 = ((bf16[32,2,256,512]{3,2,1,0:T(8,128)(2,1)}), bf16[32,2,256,512]{3,2,1,0:T(8,128)(2,1)}, u32[]{:S(2)}, u32[]{:S(2)}) async-start(bf16[32,2,256,512]{3,2,1,0:T(8,128)(2,1)} %bitcast.80), calls=%async_computation.2 | async-start | bytes 33554432 | tf_op jit(solution)/shard_map/all_to_all | solution.py:71
  711.9 25.0 %copy-start.1 = (f32[512]{0:T(512)S(1)}, f32[512]{0:T(512)}, u32[]{:S(2)}) copy-start(f32[512]{0:T(512)} %param.9) | copy-start | bytes 6148
Sparse Core Ops, SparseCore 0:
  299.3 77.5 all-gather.2
